TPU v7x, 32 devices: a whole 2x2x4 slice. The times are simulated.
32 devices in a mesh: row: 2 (over core), col: 16 (over z, y, x).
Axes of the slice: x: 2, y: 2, z: 4, core: 2. Of those that a mesh axis runs over, the one named last changes fastest.
Arguments:
- spectra: bfloat16 [2, 512, 20480], P(None, None, ('row', 'col')), may hold values from -6 to 6
Outputs:
- cross: bfloat16 [2, 20480, 20480], P(None, 'row', 'col')
All inputs are finite; a program needn't handle non-finite values.
Results may differ from a plain program's by a relative error of at most 0.0049.
Values may be sent and summed in bfloat16 or wider, within the bound.
A program may use at most 256 MiB of HBM per device.

v0:
```python
import jax
import jax.numpy as jnp
from jax import lax
from jax.sharding import PartitionSpec as P


def spread(block, axis, source):
    block = jnp.where(lax.axis_index(axis) == source, block, jnp.zeros_like(block))
    return lax.psum(block, axis)


def contract(left, right):
    return lax.dot_general(
        left, right, (((0,), (0,)), ((), ())), preferred_element_type=jnp.float32
    )


def cross_products(row_block, column_panel, segments):
    real_part = contract(row_block[0], column_panel[0]) + contract(row_block[1], column_panel[1])
    imag_part = contract(row_block[1], column_panel[0]) - contract(row_block[0], column_panel[1])
    result = jnp.stack([real_part, imag_part])
    return (result / segments).astype(jnp.bfloat16)


def per_device(spectra):
    floats = spectra.astype(jnp.float32)
    magnitude = jnp.sqrt(floats[0] * floats[0] + floats[1] * floats[1])
    whitened = (floats / jnp.maximum(magnitude, 1.0)).astype(jnp.bfloat16)
    row_count = lax.axis_size("row")
    col_count = lax.axis_size("col")
    channels = spectra.shape[2] * row_count * col_count
    row_width = channels // row_count
    panel_width = channels // col_count
    row_block = lax.all_gather(whitened, "col", axis=2, tiled=True)
    first_channel = lax.axis_index("col") * panel_width
    offset = first_channel % row_width
    root_row = first_channel // row_width
    own_slice = lax.dynamic_slice_in_dim(row_block, offset, panel_width, 2)
    column_panel = spread(own_slice, "row", root_row)
    return cross_products(row_block, column_panel, spectra.shape[1])


def solution(mesh):
    in_specs = (P(None, None, ("row", "col")),)
    out_specs = P(None, "row", "col")
    return jax.shard_map(
        per_device, mesh=mesh, in_specs=in_specs, out_specs=out_specs, check_vma=False
    )
```

profile of v0, /device:TPU:0, one launch (start us, length us, event | category | flops | bytes accessed | tf_op | source)
XLA Modules:
  0.0 474.0 jit_solution(18265915802104516297)
XLA Ops:
  6.5 0.0 all-gather.2.cloned.1.call-start
  6.5 1.5 convert_element_type.9
  8.0 0.0 copy-start
  8.0 0.5 fusion.6
  8.5 0.8 copy-done
  9.3 1.4 divide_convert_fusion
  10.7 0.0 all-gather.2.cloned.1.call-update
  10.8 0.0 all-reduce.2.cloned.1.call-start
  10.8 254.9 %all-gather.2.cloned.1.call-done = bf16[2,512,10240]{2,1,0:T(8,128)(2,1)} async-done(((bf16[2,512,640]{2,1,0:T(8,128)(2,1)}), bf16[2,512,10240]{2,1,0:T(8,128)(2,1)}) %all-gather.2.cloned.1.call-update) | async-done | bytes 20971536 | tf_op jit(solution)/shard_map/all_gather | solution.py:34
  265.8 4.8 %dynamic-slice_select_fusion = bf16[2,512,1280]{2,1,0:T(8,128)(2,1)} fusion(bf16[2,512,10240]{2,1,0:T(8,128)(2,1)} %all-gather.2.cloned.1.call-done, s32[]{:T(128)S(6)} %select_n.25, pred[]{:T(512)S(6)} %eq.5), kind=kLoop, calls=%fused_computation.8 | loop fusion | flops 1310720 | bytes 5242885 | tf_op jit(solution)/shard_map/jit(_where)/select_n | solution.py:8
  270.6 0.0 all-reduce.2.cloned.1.call-update
  270.6 20.5 %all-reduce.2.cloned.1.call-done = bf16[2,512,1280]{2,1,0:T(8,128)(2,1)} async-done(((bf16[2,512,1280]{2,1,0:T(8,128)(2,1)}), bf16[2,512,1280]{2,1,0:T(8,128)(2,1)}) %all-reduce.2.cloned.1.call-update) | async-done | bytes 2621456 | tf_op jit(solution)/shard_map/psum | solution.py:9
  291.1 0.0 copy-start.1
  291.1 26.2 %fusion.2 = f32[10240,1280]{1,0:T(8,128)} fusion(bf16[2,512,10240]{2,1,0:T(8,128)(2,1)} %all-gather.2.cloned.1.call-done, bf16[2,512,1280]{2,1,0:T(8,128)(2,1)} %all-reduce.2.cloned.1.call-done), kind=kOutput, calls=%fused_computation.7 | convolution fusion | flops 13421772800 | bytes 64225280 | tf_op jit(solution)/shard_map/dot_general | solution.py:13
  317.3 0.0 copy-done.1
  317.3 25.1 %fusion.1 = f32[10240,1280]{1,0:T(8,128)} fusion(bf16[2,512,10240]{2,1,0:T(8,128)(2,1)} %all-gather.2.cloned.1.call-done, bf16[2,512,1280]{2,1,0:T(8,128)(2,1)S(1)} %copy-done.1), kind=kOutput, calls=%fused_computation.6 | convolution fusion | flops 13421772800 | bytes 64225280 | tf_op jit(solution)/shard_map/dot_general | solution.py:13
  342.4 36.5 %subtract_bitcast_fusion = f32[1,10240,1280]{2,1,0:T(8,128)} fusion(f32[10240,1280]{1,0:T(8,128)} %fusion.2, bf16[2,512,10240]{2,1,0:T(8,128)(2,1)} %all-gather.2.cloned.1.call-done, bf16[2,512,1280]{2,1,0:T(8,128)(2,1)S(1)} %copy-done.1), kind=kOutput, calls=%fused_computation.2 | convolution fusion | flops 13434880000 | bytes 116654080 | tf_op jit(solution)/shard_map/dot_general | solution.py:13
  378.9 36.4 %add_bitcast_fusion = f32[1,10240,1280]{2,1,0:T(8,128)} fusion(f32[10240,1280]{1,0:T(8,128)} %fusion.1, bf16[2,512,10240]{2,1,0:T(8,128)(2,1)} %all-gather.2.cloned.1.call-done, bf16[2,512,1280]{2,1,0:T(8,128)(2,1)S(1)} %copy-done.1), kind=kOutput, calls=%fused_computation.3 | convolution fusion | flops 13434880000 | bytes 116654080 | tf_op jit(solution)/shard_map/dot_general | solution.py:13
  415.3 51.8 %fusion = bf16[2,10240,1280]{2,1,0:T(8,128)(2,1)} fusion(f32[1,10240,1280]{2,1,0:T(8,128)} %subtract_bitcast_fusion, f32[1,10240,1280]{2,1,0:T(8,128)} %add_bitcast_fusion), kind=kLoop, calls=%fused_computation.1 | loop fusion | flops 78643200 | bytes 157286400 | tf_op jit(solution)/shard_map/convert_element_type | solution.py:22
Async XLA Ops:
  6.5 259.2 %all-gather.2.cloned.1.call-start = ((), (), s32[]{:S(2)}) async-start(), calls=%async_computation | async-start | bytes 22282240 | tf_op jit(solution)/shard_map/all_gather | solution.py:34
  8.0 1.3 copy-start
  10.8 280.4 %all-reduce.2.cloned.1.call-start = ((), (), s32[]{:S(2)}) async-start(), calls=%async_computation.1 | async-start | bytes 5242880 | tf_op jit(solution)/shard_map/psum | solution.py:9
  291.1 26.2 %copy-start.1 = (bf16[2,512,1280]{2,1,0:T(8,128)(2,1)S(1)}, bf16[2,512,1280]{2,1,0:T(8,128)(2,1)}, u32[]{:S(2)}) copy-start(bf16[2,512,1280]{2,1,0:T(8,128)(2,1)} %all-reduce.2.cloned.1.call-done) | copy-start | bytes 7864324
Sparse Core Ops, SparseCore 0:
  10.9 254.8 all-gather.1
  270.7 20.3 all-reduce.1
where the time goes:
time: 474 us
  waiting for transfers between devices  276 us (58%)
  matrix products  124 us (26%)
  other arithmetic  59.9 us (13%)
  between operations  13.5 us (3%)
    all_gather x1, waiting for transfers between devices, per_device(): row_block = lax.all_gather(whitened, 'col', axis=2, tiled=True)  255 us
    dot_general x4, matrix products, contract(): lax.dot_general(left, right, (((0,), (0,)), ((), ())), preferred_element_...  124 us
    convert_element_type x1, other arithmetic, cross_products(): return (result / segments).astype(jnp.bfloat16)  51.8 us
    psum x1, waiting for transfers between devices, spread(): return lax.psum(block, axis)  20.5 us
  transfers between devices with their start and end apart: 2, of which 2 were waited for; matrix products, arithmetic and copies ran while one was open for 0% of the time, Pallas kernels for 0%

commit v1 on v0

v1 whole, which is shorter than its diff:
```python
import functools

import jax
import jax.numpy as jnp
from jax import lax
from jax.experimental import pallas as pl
from jax.experimental.pallas import tpu as pltpu
from jax.sharding import PartitionSpec as P


def whiten(spectra):
    floats = spectra.astype(jnp.float32)
    magnitude = jnp.sqrt(floats[0] * floats[0] + floats[1] * floats[1])
    return (floats / jnp.maximum(magnitude, 1.0)).astype(jnp.bfloat16)


def contract(left, right):
    return lax.dot_general(
        left, right, (((0,), (0,)), ((), ())), preferred_element_type=jnp.float32
    )


def cross_products(row_block, column_panel, segments):
    real_part = contract(row_block[0], column_panel[0]) + contract(row_block[1], column_panel[1])
    imag_part = contract(row_block[1], column_panel[0]) - contract(row_block[0], column_panel[1])
    result = jnp.stack([real_part, imag_part])
    return (result / segments).astype(jnp.bfloat16)


def per_device_general(spectra):
    whitened = whiten(spectra)
    row_count = lax.axis_size("row")
    col_count = lax.axis_size("col")
    channels = spectra.shape[2] * row_count * col_count
    row_width = channels // row_count
    panel_width = channels // col_count
    row_block = lax.all_gather(whitened, "col", axis=2, tiled=True)
    first_channel = lax.axis_index("col") * panel_width
    offset = first_channel % row_width
    root_row = first_channel // row_width
    own_slice = lax.dynamic_slice_in_dim(row_block, offset, panel_width, 2)
    here = lax.axis_index("row") == root_row
    column_panel = lax.psum(jnp.where(here, own_slice, jnp.zeros_like(own_slice)), "row")
    return cross_products(row_block, column_panel, spectra.shape[1])


TILE = 256


def multiply_kernel(count, scale, owners, *refs):
    lefts = refs[: 2 * count]
    panel = refs[2 * count]
    out, held = refs[-2], refs[-1]
    segments = lefts[0].shape[1]
    step = pl.program_id(0)
    for block in range(count):

        @pl.when(step == block)
        def _():
            held[:, :segments] = lefts[2 * block][0].T
            held[:, segments:] = lefts[2 * block + 1][0].T

    for part in range(2):
        for first in range(0, out.shape[2], TILE):
            columns = slice(first, first + TILE)
            product = jnp.dot(
                held[...], panel[part, :, columns], preferred_element_type=jnp.float32
            )
            out[part, :, columns] = (product * scale).astype(out.dtype)


def multiply(total, blocks, panel, rows):
    count = len(blocks)
    segments, width = blocks[0][1][0].shape[1:]
    panel_width = panel.shape[2]
    owners = jnp.stack([jnp.asarray(owner, jnp.int32) for owner, _, _ in blocks])
    operands, specs = [], []
    for _, *parts in blocks:
        for array, index in parts:
            operands.append(array)
            specs.append(
                pl.BlockSpec(
                    (1, segments, width),
                    lambda i, owners, index=index: (index, 0, 0),
                    pipeline_mode=pl.Buffered(1),
                )
            )
    operands.append(panel)
    specs.append(
        pl.BlockSpec(panel.shape, lambda i, owners: (0, 0, 0), pipeline_mode=pl.Buffered(1))
    )
    aliases = {}
    if total is not None:
        aliases = {1 + len(operands): 0}
        operands.append(total)
        specs.append(pl.BlockSpec(memory_space=pl.ANY))
    return pl.pallas_call(
        functools.partial(multiply_kernel, count, 1.0 / segments),
        out_shape=jax.ShapeDtypeStruct((2, rows, panel_width), jnp.bfloat16),
        grid_spec=pltpu.PrefetchScalarGridSpec(
            num_scalar_prefetch=1,
            grid=(count,),
            in_specs=specs,
            out_specs=pl.BlockSpec((2, width, panel_width), lambda i, owners: (0, owners[i], 0)),
            scratch_shapes=[pltpu.VMEM((width, 2 * segments), jnp.bfloat16)],
        ),
        input_output_aliases=aliases,
        compiler_params=pltpu.CompilerParams(vmem_limit_bytes=40 * 2**20),
        cost_estimate=pl.CostEstimate(
            flops=count * 2 * width * 2 * segments * 2 * panel_width,
            bytes_accessed=count * 4 * width * (segments + panel_width) + 2 * panel.size,
            transcendentals=0,
        ),
    )(owners, *operands)


def per_device_block(spectra):
    segments, width = spectra.shape[1:]
    row_count, col_count = lax.axis_size("row"), lax.axis_size("col")
    rows = width * col_count
    devices = row_count * col_count
    core, me = lax.axis_index("row"), lax.axis_index("col")
    z = me // 4
    inner = (z == 1) | (z == 2)

    def chips(z_pairs, change):
        return [
            (a * 4 + k, b * 4 + (k ^ change)) for a, b in z_pairs for k in range(4)
        ]

    levels = [(k, k) for k in range(4)]
    x_pairs, y_pairs = chips(levels, 1), chips(levels, 2)
    near_pairs = chips([(k, k ^ 1) for k in range(4)], 0)
    middle_pairs = chips([(1, 2), (2, 1)], 0)
    end_pairs = chips([(1, 0), (2, 3)], 0)

    def send(array, pairs):
        return lax.ppermute(array, "col", pairs)

    own = whiten(spectra)

    panel_pairs = [
        (f, (f % row_count) * col_count + f // row_count) for f in range(devices)
    ]
    mine = lax.ppermute(own, ("row", "col"), panel_pairs)
    other = lax.ppermute(mine, "row", [(0, 1), (1, 0)])
    first = jnp.where(core == 0, mine, other)
    second = jnp.where(core == 0, other, mine)
    panel = jnp.concatenate([first, second], axis=2)
    panel = jnp.stack(
        [
            jnp.concatenate([panel[0], panel[1]], axis=0),
            jnp.concatenate([-panel[1], panel[0]], axis=0),
        ]
    )

    def plane(array):
        by_x, by_y = send(array, x_pairs), send(array, y_pairs)
        return by_x, by_y

    def corner(by_x, by_y):
        return send(by_x[:1], y_pairs), send(by_y[1:], x_pairs)

    def whole(array):
        return (array, 0), (array, 1)

    def halves(pair):
        return (pair[0], 0), (pair[1], 0)

    near = send(own, near_pairs)
    far_middle = send(own, middle_pairs)
    far = jnp.where(inner, far_middle, send(far_middle, end_pairs))
    last_middle = send(near, middle_pairs)
    last = jnp.where(inner, last_middle, send(last_middle, end_pairs))

    own_x, own_y = plane(own)
    own_xy = corner(own_x, own_y)
    near_x, near_y = plane(near)
    far_x, far_y = plane(far)
    last_x, last_y = plane(last)
    last_xy = corner(last_x, last_y)
    near_xy = tuple(send(part, near_pairs) for part in own_xy)
    far_xy = []
    for part in own_xy:
        middle = send(part, middle_pairs)
        far_xy.append(jnp.where(inner, middle, send(middle, end_pairs)))

    k = me % 4
    near_z = z ^ 1
    far_z = jnp.where(z < 2, 2, 1)
    last_z = jnp.where(z < 2, 3, 0)

    def owner(level, change):
        return level * 4 + (k ^ change)

    steps = [
        [(owner(z, 0), *whole(own)), (owner(z, 1), *whole(own_x)), (owner(z, 2), *whole(own_y))],
        [
            (owner(z, 3), *halves(own_xy)),
            (owner(near_z, 0), *whole(near)),
            (owner(near_z, 1), *whole(near_x)),
            (owner(near_z, 2), *whole(near_y)),
        ],
        [
            (owner(far_z, 0), *whole(far)),
            (owner(far_z, 1), *whole(far_x)),
            (owner(far_z, 2), *whole(far_y)),
            (owner(near_z, 3), *halves(near_xy)),
        ],
        [
            (owner(last_z, 0), *whole(last)),
            (owner(last_z, 1), *whole(last_x)),
            (owner(last_z, 2), *whole(last_y)),
        ],
        [(owner(far_z, 3), *halves(far_xy)), (owner(last_z, 3), *halves(last_xy))],
    ]
    total = None
    for blocks in steps:
        total = multiply(total, blocks, panel, rows)
    return total


def solution(mesh):
    in_specs = (P(None, None, ("row", "col")),)
    out_specs = P(None, "row", "col")
    fits = mesh.shape["row"] == 2 and mesh.shape["col"] == 16
    body = per_device_block if fits else per_device_general
    return jax.shard_map(
        body, mesh=mesh, in_specs=in_specs, out_specs=out_specs, check_vma=False
    )
```

time: 474 us -> 254 us (0.54)
  waiting for transfers between devices: 276 us -> 90.8 us
  matrix products: 124 us -> 0 us
  Pallas kernels: 0 us -> 78.7 us
  starting transfers between devices: 0.04 us -> 74.1 us
  other arithmetic: 59.9 us -> 6.54 us
  between operations: 13.5 us -> 0.2 us
    all_gather x1 -> x0, waiting for transfers between devices: 255 us -> none  [per_device(): row_block = lax.all_gather(whitened, 'col', axis=2, tiled=True)]
    dot_general x4 -> x0, matrix products: 124 us -> none  [contract(): lax.dot_general(left, right, (((0,), (0,)), ((), ())), preferred_element_...]
    ppermute x0 -> x25, waiting for transfers between devices: none -> 90.8 us  [the longest x23 90.8 us: send(): return lax.ppermute(array, 'col', pairs)]
    pallas_call x0 -> x5, Pallas kernels: none -> 78.7 us  [multiply(): pl.pallas_call(functools.partial(multiply_kernel, count, 1.0 / segments),...]
    ppermute x0 -> x25, starting transfers between devices: none -> 74.1 us  [the longest x1 36.2 us: per_device_block(): other = lax.ppermute(mine, 'row', [(0, 1), (1, 0)])]
    convert_element_type x3 -> x2, other arithmetic: 54.6 us -> 1.84 us  [the longest x1 1.49 us: whiten(): floats = spectra.astype(jnp.float32)]
    psum x1 -> x0, waiting for transfers between devices: 20.5 us -> none  [spread(): return lax.psum(block, axis)]
  transfers between devices with their start and end apart: 2 -> 25, of which waited for: 2 -> 7; matrix products, arithmetic and copies ran while one was open for 0% -> 3% of each run, Pallas kernels for 0% -> 27%
where the time goes in v1:
time: 254 us; the launch traced here: 253 us
  waiting for transfers between devices  90.8 us (36%)
  Pallas kernels  78.7 us (31%)
  starting transfers between devices  74.1 us (29%)
  other arithmetic  6.54 us (3%)
  local copies, waits for them, and re-layouts  2.99 us (1%)
    ppermute x23, waiting for transfers between devices, send(): return lax.ppermute(array, 'col', pairs)  90.8 us
    pallas_call x5, Pallas kernels, multiply(): pl.pallas_call(functools.partial(multiply_kernel, count, 1.0 / segments),...  78.7 us
    ppermute x1, starting transfers between devices, per_device_block(): other = lax.ppermute(mine, 'row', [(0, 1), (1, 0)])  36.2 us
    ppermute x23, starting transfers between devices, send(): return lax.ppermute(array, 'col', pairs)  36.2 us
  transfers between devices with their start and end apart: 25, of which 7 were waited for; matrix products, arithmetic and copies ran while one was open for 3% of the time, Pallas kernels for 27%

profile of v1, /device:TPU:0, one launch (start us, length us, event | category | flops | bytes accessed | tf_op | source)
XLA Modules:
  0.0 253.3 jit_solution(8763292419170600621)
XLA Ops:
  0.0 1.5 convert_element_type.6
  1.5 0.5 fusion.6
  2.0 0.8 copy-done
  2.8 0.4 divide_convert_fusion.refs_0_.refs_1_
  3.2 1.7 collective-permute-start.15
  4.9 4.6 %collective-permute-start.4 = (bf16[2,512,640]{2,1,0:T(8,128)(2,1)S(1)}, bf16[2,512,640]{2,1,0:T(8,128)(2,1)S(1)}, u32[]{:S(2)}, u32[]{:S(2)}) collective-permute-start(bf16[2,512,640]{2,1,0:T(8,128)(2,1)S(1)} %divide_convert_fusion.refs_0_.refs_1_), channel_id=1, source_target_pairs={{0,2},{1,3},{2,0},{3,1},{4,6},{5,7},{6,4},{7,5},{8,10},{9,11},{10,... | collective-permute-start | bytes 3932168 | tf_op jit(solution)/shard_map/ppermute | solution.py:138
  9.6 1.6 collective-permute-start.8
  11.2 1.8 collective-permute-start.17
  13.0 36.2 %collective-permute-start.16 = (bf16[2,512,640]{2,1,0:T(8,128)(2,1)}, bf16[2,512,640]{2,1,0:T(8,128)(2,1)}, u32[]{:S(2)}, u32[]{:S(2)}) collective-permute-start(bf16[2,512,640]{2,1,0:T(8,128)(2,1)} %collective-permute-done.15), channel_id=1, source_target_pairs={{0,16},{16,0},{1,17},{17,1},{2,18},{18,2},{3,19},{19,3},{4,20},{20... | collective-permute-start | bytes 3932168 | tf_op jit(solution)/shard_map/ppermute | solution.py:146
  49.1 17.0 %collective-permute-done.4.refs_4_.refs_5_ = bf16[2,512,640]{2,1,0:T(8,128)(2,1)S(1)} collective-permute-done((bf16[2,512,640]{2,1,0:T(8,128)(2,1)S(1)}, bf16[2,512,640]{2,1,0:T(8,128)(2,1)S(1)}, u32[]{:S(2)}, u32[]{:S(2)}) %collective-permute-start.4) | collective-permute-done | bytes 1310752 | tf_op jit(solution)/shard_map/ppermute | solution.py:138
  66.1 0.9 slice.39
  67.0 1.2 collective-permute-start.5
  68.5 1.2 slice.38
  69.7 1.4 collective-permute-start.1
  71.1 2.0 collective-permute-start.23
  73.1 0.1 collective-permute-start.24
  73.2 11.6 %collective-permute-done.5.refs_1_ = bf16[1,512,640]{2,1,0:T(8,128)(2,1)S(1)} collective-permute-done((bf16[1,512,640]{2,1,0:T(8,128)(2,1)}, bf16[1,512,640]{2,1,0:T(8,128)(2,1)S(1)}, u32[]{:S(2)}, u32[]{:S(2)}) %collective-permute-start.5) | collective-permute-done | bytes 655392 | tf_op jit(solution)/shard_map/ppermute | solution.py:138
  84.7 1.3 collective-permute-start.18
  86.0 0.7 collective-permute-start.6
  86.8 2.0 broadcast_select_fusion
  88.7 0.3 fusion.7
  89.1 0.1 fusion.1
  89.2 0.5 maximum_bitcast_fusion
  89.7 0.7 collective-permute-start.9
  90.4 0.5 pad_maximum_fusion.refs_6_.refs_8_.refs_4_
  90.9 25.5 %collective-permute-done.18 = bf16[2,512,640]{2,1,0:T(8,128)(2,1)S(1)} collective-permute-done((bf16[2,512,640]{2,1,0:T(8,128)(2,1)}, bf16[2,512,640]{2,1,0:T(8,128)(2,1)S(1)}, u32[]{:S(2)}, u32[]{:S(2)}) %collective-permute-start.18) | collective-permute-done | bytes 1310752 | tf_op jit(solution)/shard_map/ppermute | solution.py:138
  116.4 0.7 collective-permute-start.2
  117.1 1.3 collective-permute-start.7
  118.4 15.6 %shard_map.17.refs_9_ = bf16[2,10240,1280]{2,1,0:T(8,128)(2,1)} custom-call(s32[3]{0:T(128)S(1)} %pad_add_fusion.4.owners, bf16[2,512,640]{2,1,0:T(8,128)(2,1)S(1)} %divide_convert_fusion.refs_0_.refs_1_, bf16[2,512,640]{2,1,0:T(8,128)(2,1)S(1)} %divide_convert_fusion.refs_0_.refs_1_, bf16[2,512,640]{2,1,0:T(8,128)(2,1)} %collective-permute-done.refs_2_.refs_3_, ...), custom_call_target="tpu_custom_call" | custom-call | flops 10066329600 | bytes 19005440 | tf_op jit(solution)/shard_map/pallas_call | solution.py:97
  134.1 1.3 collective-permute-start.10
  135.4 0.2 broadcast_select_fusion.2.refs_0_.refs_1_
  135.6 4.5 %collective-permute-start.21 = (bf16[1,512,640]{2,1,0:T(8,128)(2,1)S(1)}, bf16[1,512,640]{2,1,0:T(8,128)(2,1)S(1)}, u32[]{:S(2)}, u32[]{:S(2)}) collective-permute-start(bf16[1,512,640]{2,1,0:T(8,128)(2,1)S(1)} %collective-permute-done.1.refs_0_), channel_id=1, source_target_pairs={{0,4},{1,5},{2,6},{3,7},{4,0},{5,1},{6,2},{7,3},{8,12},{9,13},{10,... | collective-permute-start | bytes 1966088 | tf_op jit(solution)/shard_map/ppermute | solution.py:138
  140.1 1.4 collective-permute-start.19
  141.5 0.9 collective-permute-start.20
  142.4 1.5 collective-permute-start.3
  143.9 19.7 %shard_map.18.refs_9_ = bf16[2,10240,1280]{2,1,0:T(8,128)(2,1)} custom-call(s32[4]{0:T(128)S(1)} %pad_add_fusion.3.owners, bf16[1,512,640]{2,1,0:T(8,128)(2,1)S(1)} %collective-permute-done.1.refs_0_, bf16[1,512,640]{2,1,0:T(8,128)(2,1)S(1)} %collective-permute-done.5.refs_1_, ...), custom_call_target="tpu_custom_call", output_to_operand_aliasing={{}: (10, {})} | custom-call | flops 13421772800 | bytes 23592960 | tf_op jit(solution)/shard_map/pallas_call | solution.py:97
  163.6 4.5 %collective-permute-done.10 = bf16[2,512,640]{2,1,0:T(8,128)(2,1)S(1)} collective-permute-done((bf16[2,512,640]{2,1,0:T(8,128)(2,1)S(1)}, bf16[2,512,640]{2,1,0:T(8,128)(2,1)S(1)}, u32[]{:S(2)}, u32[]{:S(2)}) %collective-permute-start.10) | collective-permute-done | bytes 1310752 | tf_op jit(solution)/shard_map/ppermute | solution.py:138
  168.1 3.4 %collective-permute-start.22 = (bf16[1,512,640]{2,1,0:T(8,128)(2,1)S(1)}, bf16[1,512,640]{2,1,0:T(8,128)(2,1)S(1)}, u32[]{:S(2)}, u32[]{:S(2)}) collective-permute-start(bf16[1,512,640]{2,1,0:T(8,128)(2,1)S(1)} %collective-permute-done.5.refs_1_), channel_id=1, source_target_pairs={{0,4},{1,5},{2,6},{3,7},{4,0},{5,1},{6,2},{7,3},{8,12},{9,13},{10,... | collective-permute-start | bytes 1966088 | tf_op jit(solution)/shard_map/ppermute | solution.py:138
  171.6 0.1 broadcast_select_fusion.3.refs_0_.refs_1_
  171.7 10.4 %collective-permute-done.21.refs_6_ = bf16[1,512,640]{2,1,0:T(8,128)(2,1)S(1)} collective-permute-done((bf16[1,512,640]{2,1,0:T(8,128)(2,1)S(1)}, bf16[1,512,640]{2,1,0:T(8,128)(2,1)S(1)}, u32[]{:S(2)}, u32[]{:S(2)}) %collective-permute-start.21) | collective-permute-done | bytes 655392 | tf_op jit(solution)/shard_map/ppermute | solution.py:138
  182.1 1.4 collective-permute-start.11
  183.6 12.6 %collective-permute-done.3 = bf16[1,512,640]{2,1,0:T(8,128)(2,1)S(1)} collective-permute-done((bf16[1,512,640]{2,1,0:T(8,128)(2,1)S(1)}, bf16[1,512,640]{2,1,0:T(8,128)(2,1)S(1)}, u32[]{:S(2)}, u32[]{:S(2)}) %collective-permute-start.3) | collective-permute-done | bytes 655392 | tf_op jit(solution)/shard_map/ppermute | solution.py:138
  196.2 1.8 collective-permute-start.13
  198.1 9.2 %collective-permute-done.22.refs_7_ = bf16[1,512,640]{2,1,0:T(8,128)(2,1)S(1)} collective-permute-done((bf16[1,512,640]{2,1,0:T(8,128)(2,1)S(1)}, bf16[1,512,640]{2,1,0:T(8,128)(2,1)S(1)}, u32[]{:S(2)}, u32[]{:S(2)}) %collective-permute-start.22) | collective-permute-done | bytes 655392 | tf_op jit(solution)/shard_map/ppermute | solution.py:138
  207.2 18.4 %shard_map.19.refs_7_ = bf16[2,10240,1280]{2,1,0:T(8,128)(2,1)} custom-call(s32[4]{0:T(128)S(1)} %pad_add_fusion.2.owners, bf16[2,512,640]{2,1,0:T(8,128)(2,1)S(1)} %broadcast_select_fusion.2.refs_0_.refs_1_, bf16[2,512,640]{2,1,0:T(8,128)(2,1)S(1)} %broadcast_select_fusion.2.refs_0_.refs_1_, ...), custom_call_target="tpu_custom_call", output_to_operand_aliasing={{}: (10, {})} | custom-call | flops 13421772800 | bytes 23592960 | tf_op jit(solution)/shard_map/pallas_call | solution.py:97
  225.7 2.5 collective-permute-start.12
  228.3 14.4 %shard_map.20.refs_5_ = bf16[2,10240,1280]{2,1,0:T(8,128)(2,1)} custom-call(s32[3]{0:T(128)S(1)} %pad_add_fusion.1.owners, bf16[2,512,640]{2,1,0:T(8,128)(2,1)S(1)} %broadcast_select_fusion.3.refs_0_.refs_1_, bf16[2,512,640]{2,1,0:T(8,128)(2,1)S(1)} %broadcast_select_fusion.3.refs_0_.refs_1_, ...), custom_call_target="tpu_custom_call", output_to_operand_aliasing={{}: (8, {})} | custom-call | flops 10066329600 | bytes 19005440 | tf_op jit(solution)/shard_map/pallas_call | solution.py:97
  242.7 10.5 %shard_map.21 = bf16[2,10240,1280]{2,1,0:T(8,128)(2,1)} custom-call(s32[2]{0:T(128)S(1)} %pad_add_fusion.owners, bf16[1,512,640]{2,1,0:T(8,128)(2,1)S(1)} %broadcast_select_fusion.5.refs_0_, bf16[1,512,640]{2,1,0:T(8,128)(2,1)S(1)} %broadcast_select_fusion.4.refs_1_, ...), custom_call_target="tpu_custom_call", output_to_operand_aliasing={{}: (6, {})} | custom-call | flops 6710886400 | bytes 14417920 | tf_op jit(solution)/shard_map/pallas_call | solution.py:97
  (30 shorter events, 0.8 us)
Async XLA Ops:
  1.5 1.3 copy-start
  3.2 9.8 %collective-permute-start.15 = (bf16[2,512,640]{2,1,0:T(8,128)(2,1)S(1)}, bf16[2,512,640]{2,1,0:T(8,128)(2,1)}, u32[]{:S(2)}, u32[]{:S(2)}) collective-permute-start(bf16[2,512,640]{2,1,0:T(8,128)(2,1)S(1)} %divide_convert_fusion.refs_0_.refs_1_), channel_id=1, source_target_pairs={{0,0},{1,16},{2,1},{3,17},{4,2},{5,18},{6,3},{7,19},{8,4},{9,20},{... | collective-permute-start | bytes 3932168 | tf_op jit(solution)/shard_map/ppermute | solution.py:145
  4.9 61.2 %collective-permute-start.4 = (bf16[2,512,640]{2,1,0:T(8,128)(2,1)S(1)}, bf16[2,512,640]{2,1,0:T(8,128)(2,1)S(1)}, u32[]{:S(2)}, u32[]{:S(2)}) collective-permute-start(bf16[2,512,640]{2,1,0:T(8,128)(2,1)S(1)} %divide_convert_fusion.refs_0_.refs_1_), channel_id=1, source_target_pairs={{0,2},{1,3},{2,0},{3,1},{4,6},{5,7},{6,4},{7,5},{8,10},{9,11},{10,... | collective-permute-start | bytes 3932168 | tf_op jit(solution)/shard_map/ppermute | solution.py:138
  9.6 59.0 %collective-permute-start = (bf16[2,512,640]{2,1,0:T(8,128)(2,1)S(1)}, bf16[2,512,640]{2,1,0:T(8,128)(2,1)}, u32[]{:S(2)}, u32[]{:S(2)}) collective-permute-start(bf16[2,512,640]{2,1,0:T(8,128)(2,1)S(1)} %divide_convert_fusion.refs_0_.refs_1_), channel_id=1, source_target_pairs={{0,1},{1,0},{2,3},{3,2},{4,5},{5,4},{6,7},{7,6},{8,9},{9,8},{10,11... | collective-permute-start | bytes 3932168 | tf_op jit(solution)/shard_map/ppermute | solution.py:138
  9.6 61.5 %collective-permute-start.8 = (bf16[2,512,640]{2,1,0:T(8,128)(2,1)S(1)}, bf16[2,512,640]{2,1,0:T(8,128)(2,1)}, u32[]{:S(2)}, u32[]{:S(2)}) collective-permute-start(bf16[2,512,640]{2,1,0:T(8,128)(2,1)S(1)} %divide_convert_fusion.refs_0_.refs_1_), channel_id=1, source_target_pairs={{0,4},{1,5},{2,6},{3,7},{4,0},{5,1},{6,2},{7,3},{8,12},{9,13},{10,... | collective-permute-start | bytes 3932168 | tf_op jit(solution)/shard_map/ppermute | solution.py:138
  11.2 61.9 %collective-permute-start.17 = (bf16[2,512,640]{2,1,0:T(8,128)(2,1)S(1)}, bf16[2,512,640]{2,1,0:T(8,128)(2,1)}, u32[]{:S(2)}, u32[]{:S(2)}) collective-permute-start(bf16[2,512,640]{2,1,0:T(8,128)(2,1)S(1)} %divide_convert_fusion.refs_0_.refs_1_), channel_id=1, source_target_pairs={{4,8},{5,9},{6,10},{7,11},{8,4},{9,5},{10,6},{11,7},{20,24},{21,25... | collective-permute-start | bytes 3932168 | tf_op jit(solution)/shard_map/ppermute | solution.py:138
  13.0 73.1 %collective-permute-start.16 = (bf16[2,512,640]{2,1,0:T(8,128)(2,1)}, bf16[2,512,640]{2,1,0:T(8,128)(2,1)}, u32[]{:S(2)}, u32[]{:S(2)}) collective-permute-start(bf16[2,512,640]{2,1,0:T(8,128)(2,1)} %collective-permute-done.15), channel_id=1, source_target_pairs={{0,16},{16,0},{1,17},{17,1},{2,18},{18,2},{3,19},{19,3},{4,20},{20... | collective-permute-start | bytes 3932168 | tf_op jit(solution)/shard_map/ppermute | solution.py:146
  67.0 17.8 %collective-permute-start.5 = (bf16[1,512,640]{2,1,0:T(8,128)(2,1)}, bf16[1,512,640]{2,1,0:T(8,128)(2,1)S(1)}, u32[]{:S(2)}, u32[]{:S(2)}) collective-permute-start(bf16[1,512,640]{2,1,0:T(8,128)(2,1)} %slice.39), channel_id=1, source_target_pairs={{0,1},{1,0},{2,3},{3,2},{4,5},{5,4},{6,7},{7,6},{8,9},{9,8},{10,11... | collective-permute-start | bytes 1966088 | tf_op jit(solution)/shard_map/ppermute | solution.py:138
  69.7 20.0 %collective-permute-start.1 = (bf16[1,512,640]{2,1,0:T(8,128)(2,1)S(1)}, bf16[1,512,640]{2,1,0:T(8,128)(2,1)S(1)}, u32[]{:S(2)}, u32[]{:S(2)}) collective-permute-start(bf16[1,512,640]{2,1,0:T(8,128)(2,1)S(1)} %slice.38), channel_id=1, source_target_pairs={{0,2},{1,3},{2,0},{3,1},{4,6},{5,7},{6,4},{7,5},{8,10},{9,11},{10,... | collective-permute-start | bytes 1966088 | tf_op jit(solution)/shard_map/ppermute | solution.py:138
  71.1 64.5 %collective-permute-start.23 = (bf16[2,512,640]{2,1,0:T(8,128)(2,1)}, bf16[2,512,640]{2,1,0:T(8,128)(2,1)S(1)}, u32[]{:S(2)}, u32[]{:S(2)}) collective-permute-start(bf16[2,512,640]{2,1,0:T(8,128)(2,1)} %collective-permute-done.8.refs_2_.refs_3_), channel_id=1, source_target_pairs={{0,1},{1,0},{2,3},{3,2},{4,5},{5,4},{6,7},{7,6},{8,9},{9,8},{10,11... | collective-permute-start | bytes 3932168 | tf_op jit(solution)/shard_map/ppermute | solution.py:138
  73.1 67.0 %collective-permute-start.24 = (bf16[2,512,640]{2,1,0:T(8,128)(2,1)}, bf16[2,512,640]{2,1,0:T(8,128)(2,1)S(1)}, u32[]{:S(2)}, u32[]{:S(2)}) collective-permute-start(bf16[2,512,640]{2,1,0:T(8,128)(2,1)} %collective-permute-done.8.refs_2_.refs_3_), channel_id=1, source_target_pairs={{0,2},{1,3},{2,0},{3,1},{4,6},{5,7},{6,4},{7,5},{8,10},{9,11},{10,... | collective-permute-start | bytes 3932168 | tf_op jit(solution)/shard_map/ppermute | solution.py:138
  84.7 31.7 %collective-permute-start.18 = (bf16[2,512,640]{2,1,0:T(8,128)(2,1)}, bf16[2,512,640]{2,1,0:T(8,128)(2,1)S(1)}, u32[]{:S(2)}, u32[]{:S(2)}) collective-permute-start(bf16[2,512,640]{2,1,0:T(8,128)(2,1)} %collective-permute-done.17), channel_id=1, source_target_pairs={{4,0},{5,1},{6,2},{7,3},{8,12},{9,13},{10,14},{11,15},{20,16},{21,... | collective-permute-start | bytes 3932168 | tf_op jit(solution)/shard_map/ppermute | solution.py:138
  86.0 31.1 %collective-permute-start.6 = (bf16[1,512,640]{2,1,0:T(8,128)(2,1)S(1)}, bf16[1,512,640]{2,1,0:T(8,128)(2,1)S(1)}, u32[]{:S(2)}, u32[]{:S(2)}) collective-permute-start(bf16[1,512,640]{2,1,0:T(8,128)(2,1)S(1)} %collective-permute-done.5.refs_1_), channel_id=1, source_target_pairs={{4,8},{5,9},{6,10},{7,11},{8,4},{9,5},{10,6},{11,7},{20,24},{21,25... | collective-permute-start | bytes 1966088 | tf_op jit(solution)/shard_map/ppermute | solution.py:138
  89.7 44.4 %collective-permute-start.9 = (bf16[2,512,640]{2,1,0:T(8,128)(2,1)}, bf16[2,512,640]{2,1,0:T(8,128)(2,1)S(1)}, u32[]{:S(2)}, u32[]{:S(2)}) collective-permute-start(bf16[2,512,640]{2,1,0:T(8,128)(2,1)} %collective-permute-done.8.refs_2_.refs_3_), channel_id=1, source_target_pairs={{4,8},{5,9},{6,10},{7,11},{8,4},{9,5},{10,6},{11,7},{20,24},{21,25... | collective-permute-start | bytes 3932168 | tf_op jit(solution)/shard_map/ppermute | solution.py:138
  116.4 25.1 %collective-permute-start.2 = (bf16[1,512,640]{2,1,0:T(8,128)(2,1)S(1)}, bf16[1,512,640]{2,1,0:T(8,128)(2,1)S(1)}, u32[]{:S(2)}, u32[]{:S(2)}) collective-permute-start(bf16[1,512,640]{2,1,0:T(8,128)(2,1)S(1)} %collective-permute-done.1.refs_0_), channel_id=1, source_target_pairs={{4,8},{5,9},{6,10},{7,11},{8,4},{9,5},{10,6},{11,7},{20,24},{21,25... | collective-permute-start | bytes 1966088 | tf_op jit(solution)/shard_map/ppermute | solution.py:138
  117.1 25.3 %collective-permute-start.7 = (bf16[1,512,640]{2,1,0:T(8,128)(2,1)S(1)}, bf16[1,512,640]{2,1,0:T(8,128)(2,1)S(1)}, u32[]{:S(2)}, u32[]{:S(2)}) collective-permute-start(bf16[1,512,640]{2,1,0:T(8,128)(2,1)S(1)} %collective-permute-done.6), channel_id=1, source_target_pairs={{4,0},{5,1},{6,2},{7,3},{8,12},{9,13},{10,14},{11,15},{20,16},{21,... | collective-permute-start | bytes 1966088 | tf_op jit(solution)/shard_map/ppermute | solution.py:138
  134.1 34.0 %collective-permute-start.10 = (bf16[2,512,640]{2,1,0:T(8,128)(2,1)S(1)}, bf16[2,512,640]{2,1,0:T(8,128)(2,1)S(1)}, u32[]{:S(2)}, u32[]{:S(2)}) collective-permute-start(bf16[2,512,640]{2,1,0:T(8,128)(2,1)S(1)} %collective-permute-done.9), channel_id=1, source_target_pairs={{4,0},{5,1},{6,2},{7,3},{8,12},{9,13},{10,14},{11,15},{20,16},{21,... | collective-permute-start | bytes 3932168 | tf_op jit(solution)/shard_map/ppermute | solution.py:138
  135.6 46.6 %collective-permute-start.21 = (bf16[1,512,640]{2,1,0:T(8,128)(2,1)S(1)}, bf16[1,512,640]{2,1,0:T(8,128)(2,1)S(1)}, u32[]{:S(2)}, u32[]{:S(2)}) collective-permute-start(bf16[1,512,640]{2,1,0:T(8,128)(2,1)S(1)} %collective-permute-done.1.refs_0_), channel_id=1, source_target_pairs={{0,4},{1,5},{2,6},{3,7},{4,0},{5,1},{6,2},{7,3},{8,12},{9,13},{10,... | collective-permute-start | bytes 1966088 | tf_op jit(solution)/shard_map/ppermute | solution.py:138
  140.1 67.1 %collective-permute-start.19 = (bf16[2,512,640]{2,1,0:T(8,128)(2,1)S(1)}, bf16[2,512,640]{2,1,0:T(8,128)(2,1)S(1)}, u32[]{:S(2)}, u32[]{:S(2)}) collective-permute-start(bf16[2,512,640]{2,1,0:T(8,128)(2,1)S(1)} %broadcast_select_fusion.2.refs_0_.refs_1_), channel_id=1, source_target_pairs={{0,1},{1,0},{2,3},{3,2},{4,5},{5,4},{6,7},{7,6},{8,9},{9,8},{10,11... | collective-permute-start | bytes 3932168 | tf_op jit(solution)/shard_map/ppermute | solution.py:138
  141.5 65.7 %collective-permute-start.20 = (bf16[2,512,640]{2,1,0:T(8,128)(2,1)S(1)}, bf16[2,512,640]{2,1,0:T(8,128)(2,1)S(1)}, u32[]{:S(2)}, u32[]{:S(2)}) collective-permute-start(bf16[2,512,640]{2,1,0:T(8,128)(2,1)S(1)} %broadcast_select_fusion.2.refs_0_.refs_1_), channel_id=1, source_target_pairs={{0,2},{1,3},{2,0},{3,1},{4,6},{5,7},{6,4},{7,5},{8,10},{9,11},{10,... | collective-permute-start | bytes 3932168 | tf_op jit(solution)/shard_map/ppermute | solution.py:138
  142.4 53.8 %collective-permute-start.3 = (bf16[1,512,640]{2,1,0:T(8,128)(2,1)S(1)}, bf16[1,512,640]{2,1,0:T(8,128)(2,1)S(1)}, u32[]{:S(2)}, u32[]{:S(2)}) collective-permute-start(bf16[1,512,640]{2,1,0:T(8,128)(2,1)S(1)} %collective-permute-done.2), channel_id=1, source_target_pairs={{4,0},{5,1},{6,2},{7,3},{8,12},{9,13},{10,14},{11,15},{20,16},{21,... | collective-permute-start | bytes 1966088 | tf_op jit(solution)/shard_map/ppermute | solution.py:138
  168.1 39.1 %collective-permute-start.22 = (bf16[1,512,640]{2,1,0:T(8,128)(2,1)S(1)}, bf16[1,512,640]{2,1,0:T(8,128)(2,1)S(1)}, u32[]{:S(2)}, u32[]{:S(2)}) collective-permute-start(bf16[1,512,640]{2,1,0:T(8,128)(2,1)S(1)} %collective-permute-done.5.refs_1_), channel_id=1, source_target_pairs={{0,4},{1,5},{2,6},{3,7},{4,0},{5,1},{6,2},{7,3},{8,12},{9,13},{10,... | collective-permute-start | bytes 1966088 | tf_op jit(solution)/shard_map/ppermute | solution.py:138
  182.1 43.5 %collective-permute-start.11 = (bf16[2,512,640]{2,1,0:T(8,128)(2,1)S(1)}, bf16[2,512,640]{2,1,0:T(8,128)(2,1)S(1)}, u32[]{:S(2)}, u32[]{:S(2)}) collective-permute-start(bf16[2,512,640]{2,1,0:T(8,128)(2,1)S(1)} %broadcast_select_fusion.3.refs_0_.refs_1_), channel_id=1, source_target_pairs={{0,1},{1,0},{2,3},{3,2},{4,5},{5,4},{6,7},{7,6},{8,9},{9,8},{10,11... | collective-permute-start | bytes 3932168 | tf_op jit(solution)/shard_map/ppermute | solution.py:138
  196.2 32.0 %collective-permute-start.13 = (bf16[2,512,640]{2,1,0:T(8,128)(2,1)S(1)}, bf16[2,512,640]{2,1,0:T(8,128)(2,1)S(1)}, u32[]{:S(2)}, u32[]{:S(2)}) collective-permute-start(bf16[2,512,640]{2,1,0:T(8,128)(2,1)S(1)} %broadcast_select_fusion.3.refs_0_.refs_1_), channel_id=1, source_target_pairs={{0,2},{1,3},{2,0},{3,1},{4,6},{5,7},{6,4},{7,5},{8,10},{9,11},{10,... | collective-permute-start | bytes 3932168 | tf_op jit(solution)/shard_map/ppermute | solution.py:138
  225.7 17.0 %collective-permute-start.12 = (bf16[1,512,640]{2,1,0:T(8,128)(2,1)S(1)}, bf16[1,512,640]{2,1,0:T(8,128)(2,1)S(1)}, u32[]{:S(2)}, u32[]{:S(2)}) collective-permute-start(bf16[1,512,640]{2,1,0:T(8,128)(2,1)S(1)} %slice.40), channel_id=1, source_target_pairs={{0,2},{1,3},{2,0},{3,1},{4,6},{5,7},{6,4},{7,5},{8,10},{9,11},{10,... | collective-permute-start | bytes 1966088 | tf_op jit(solution)/shard_map/ppermute | solution.py:138
  228.3 14.4 %collective-permute-start.14 = (bf16[1,512,640]{2,1,0:T(8,128)(2,1)S(1)}, bf16[1,512,640]{2,1,0:T(8,128)(2,1)S(1)}, u32[]{:S(2)}, u32[]{:S(2)}) collective-permute-start(bf16[1,512,640]{2,1,0:T(8,128)(2,1)S(1)} %slice.41), channel_id=1, source_target_pairs={{0,1},{1,0},{2,3},{3,2},{4,5},{5,4},{6,7},{7,6},{8,9},{9,8},{10,11... | collective-permute-start | bytes 1966088 | tf_op jit(solution)/shard_map/ppermute | solution.py:138

commit v2 on v1

--- a/solution.py
+++ b/solution.py
@@ -194,25 +194,30 @@
         return level * 4 + (k ^ change)
 
     steps = [
-        [(owner(z, 0), *whole(own)), (owner(z, 1), *whole(own_x)), (owner(z, 2), *whole(own_y))],
-        [
+        [
+            (owner(z, 0), *whole(own)),
+            (owner(z, 1), *whole(own_x)),
+            (owner(z, 2), *whole(own_y)),
             (owner(z, 3), *halves(own_xy)),
+        ],
+        [
             (owner(near_z, 0), *whole(near)),
             (owner(near_z, 1), *whole(near_x)),
             (owner(near_z, 2), *whole(near_y)),
-        ],
-        [
             (owner(far_z, 0), *whole(far)),
+        ],
+        [
             (owner(far_z, 1), *whole(far_x)),
             (owner(far_z, 2), *whole(far_y)),
             (owner(near_z, 3), *halves(near_xy)),
-        ],
-        [
             (owner(last_z, 0), *whole(last)),
+        ],
+        [
+            (owner(far_z, 3), *halves(far_xy)),
             (owner(last_z, 1), *whole(last_x)),
             (owner(last_z, 2), *whole(last_y)),
         ],
-        [(owner(far_z, 3), *halves(far_xy)), (owner(last_z, 3), *halves(last_xy))],
+        [(owner(last_z, 3), *halves(last_xy))],
     ]
     total = None
     for blocks in steps:

time: 254 us -> 253 us (level)
  transfers between devices with their start and end apart: 25 -> 25, of which waited for: 7 -> 8; matrix products, arithmetic and copies ran while one was open for 3% -> 2% of each run, Pallas kernels for 27% -> 29%
where the time goes in v2:
time: 253 us
  waiting for transfers between devices  92.7 us (37%)
  Pallas kernels  77.5 us (31%)
  starting transfers between devices  73.1 us (29%)
  other arithmetic  6.43 us (3%)
  local copies, waits for them, and re-layouts  2.99 us (1%)
    ppermute x23, waiting for transfers between devices, send(): return lax.ppermute(array, 'col', pairs)  92.7 us
    pallas_call x5, Pallas kernels, multiply(): pl.pallas_call(functools.partial(multiply_kernel, count, 1.0 / segments),...  77.5 us
    ppermute x1, starting transfers between devices, per_device_block(): other = lax.ppermute(mine, 'row', [(0, 1), (1, 0)])  36.2 us
    ppermute x23, starting transfers between devices, send(): return lax.ppermute(array, 'col', pairs)  35.2 us
  transfers between devices with their start and end apart: 25, of which 8 were waited for; matrix products, arithmetic and copies ran while one was open for 2% of the time, Pallas kernels for 29%

profile of v2, /device:TPU:0, one launch (start us, length us, event | category | flops | bytes accessed | tf_op | source)
XLA Modules:
  0.0 252.9 jit_solution(14842531073958787681)
XLA Ops:
  0.0 1.5 convert_element_type.6
  1.5 0.5 fusion.6
  2.0 0.8 copy-done
  2.8 0.4 divide_convert_fusion.refs_0_.refs_1_
  3.2 1.7 collective-permute-start.7
  4.9 4.6 %collective-permute-start.13 = (bf16[2,512,640]{2,1,0:T(8,128)(2,1)S(1)}, bf16[2,512,640]{2,1,0:T(8,128)(2,1)S(1)}, u32[]{:S(2)}, u32[]{:S(2)}) collective-permute-start(bf16[2,512,640]{2,1,0:T(8,128)(2,1)S(1)} %divide_convert_fusion.refs_0_.refs_1_), channel_id=1, source_target_pairs={{0,2},{1,3},{2,0},{3,1},{4,6},{5,7},{6,4},{7,5},{8,10},{9,11},{10,... | collective-permute-start | bytes 3932168 | tf_op jit(solution)/shard_map/ppermute | solution.py:138
  9.6 1.6 collective-permute-start
  11.2 1.8 collective-permute-start.17
  13.0 36.2 %collective-permute-start.8 = (bf16[2,512,640]{2,1,0:T(8,128)(2,1)}, bf16[2,512,640]{2,1,0:T(8,128)(2,1)}, u32[]{:S(2)}, u32[]{:S(2)}) collective-permute-start(bf16[2,512,640]{2,1,0:T(8,128)(2,1)} %collective-permute-done.7), channel_id=1, source_target_pairs={{0,16},{16,0},{1,17},{17,1},{2,18},{18,2},{3,19},{19,3},{4,20},{20... | collective-permute-start | bytes 3932168 | tf_op jit(solution)/shard_map/ppermute | solution.py:146
  49.1 17.0 %collective-permute-done.13.refs_4_.refs_5_ = bf16[2,512,640]{2,1,0:T(8,128)(2,1)S(1)} collective-permute-done((bf16[2,512,640]{2,1,0:T(8,128)(2,1)S(1)}, bf16[2,512,640]{2,1,0:T(8,128)(2,1)S(1)}, u32[]{:S(2)}, u32[]{:S(2)}) %collective-permute-start.13) | collective-permute-done | bytes 1310752 | tf_op jit(solution)/shard_map/ppermute | solution.py:138
  66.1 0.9 slice.43
  67.0 1.2 collective-permute-start.14
  68.2 0.1 pad_add_fusion.3.owners
  68.4 0.1 pad_add_fusion.1.owners
  68.5 1.2 slice.42
  69.6 1.4 collective-permute-start.10
  71.0 2.0 collective-permute-start.23
  73.0 0.7 collective-permute-start.1
  73.8 11.0 %collective-permute-done.14.refs_7_ = bf16[1,512,640]{2,1,0:T(8,128)(2,1)S(1)} collective-permute-done((bf16[1,512,640]{2,1,0:T(8,128)(2,1)}, bf16[1,512,640]{2,1,0:T(8,128)(2,1)S(1)}, u32[]{:S(2)}, u32[]{:S(2)}) %collective-permute-start.14) | collective-permute-done | bytes 655392 | tf_op jit(solution)/shard_map/ppermute | solution.py:138
  84.7 1.3 collective-permute-start.18
  86.0 0.7 collective-permute-start.15
  86.8 2.0 broadcast_select_fusion
  88.7 0.1 fusion.1
  88.8 0.3 fusion.7
  89.2 0.5 maximum_bitcast_fusion
  89.7 0.5 pad_maximum_fusion.refs_8_.refs_6_.refs_2_
  90.2 2.6 %collective-permute-start.24 = (bf16[2,512,640]{2,1,0:T(8,128)(2,1)}, bf16[2,512,640]{2,1,0:T(8,128)(2,1)S(1)}, u32[]{:S(2)}, u32[]{:S(2)}) collective-permute-start(bf16[2,512,640]{2,1,0:T(8,128)(2,1)} %collective-permute-done.refs_0_.refs_1_), channel_id=1, source_target_pairs={{0,2},{1,3},{2,0},{3,1},{4,6},{5,7},{6,4},{7,5},{8,10},{9,11},{10,... | collective-permute-start | bytes 3932168 | tf_op jit(solution)/shard_map/ppermute | solution.py:138
  92.7 23.7 %collective-permute-done.18 = bf16[2,512,640]{2,1,0:T(8,128)(2,1)S(1)} collective-permute-done((bf16[2,512,640]{2,1,0:T(8,128)(2,1)}, bf16[2,512,640]{2,1,0:T(8,128)(2,1)S(1)}, u32[]{:S(2)}, u32[]{:S(2)}) %collective-permute-start.18) | collective-permute-done | bytes 1310752 | tf_op jit(solution)/shard_map/ppermute | solution.py:138
  116.4 0.7 collective-permute-start.11
  117.1 1.3 collective-permute-start.16
  118.4 19.7 %shard_map.17.refs_9_ = bf16[2,10240,1280]{2,1,0:T(8,128)(2,1)} custom-call(s32[4]{0:T(128)S(1)} %pad_add_fusion.3.owners, bf16[2,512,640]{2,1,0:T(8,128)(2,1)S(1)} %divide_convert_fusion.refs_0_.refs_1_, bf16[2,512,640]{2,1,0:T(8,128)(2,1)S(1)} %divide_convert_fusion.refs_0_.refs_1_, bf16[2,512,640]{2,1,0:T(8,128)(2,1)} %collective-permute-done.9.refs_2_.refs_3_, ...), custom_call_target="tpu_custom_call" | custom-call | flops 13421772800 | bytes 23592960 | tf_op jit(solution)/shard_map/pallas_call | solution.py:97
  138.1 1.3 collective-permute-start.2
  139.4 0.2 broadcast_select_fusion.2.refs_6_.refs_7_
  139.6 7.2 %collective-permute-start.21 = (bf16[1,512,640]{2,1,0:T(8,128)(2,1)S(1)}, bf16[1,512,640]{2,1,0:T(8,128)(2,1)S(1)}, u32[]{:S(2)}, u32[]{:S(2)}) collective-permute-start(bf16[1,512,640]{2,1,0:T(8,128)(2,1)S(1)} %collective-permute-done.10.refs_6_), channel_id=1, source_target_pairs={{0,4},{1,5},{2,6},{3,7},{4,0},{5,1},{6,2},{7,3},{8,12},{9,13},{10,... | collective-permute-start | bytes 1966088 | tf_op jit(solution)/shard_map/ppermute | solution.py:138
  146.8 1.8 collective-permute-start.19
  148.6 1.5 collective-permute-start.12
  150.1 19.7 %shard_map.18.refs_9_ = bf16[2,10240,1280]{2,1,0:T(8,128)(2,1)} custom-call(s32[4]{0:T(128)S(1)} %pad_add_fusion.2.owners, bf16[2,512,640]{2,1,0:T(8,128)(2,1)} %collective-permute-done.refs_0_.refs_1_, bf16[2,512,640]{2,1,0:T(8,128)(2,1)} %collective-permute-done.refs_0_.refs_1_, ...), custom_call_target="tpu_custom_call", output_to_operand_aliasing={{}: (10, {})} | custom-call | flops 13421772800 | bytes 23592960 | tf_op jit(solution)/shard_map/pallas_call | solution.py:97
  169.8 5.1 %collective-permute-done.2 = bf16[2,512,640]{2,1,0:T(8,128)(2,1)S(1)} collective-permute-done((bf16[2,512,640]{2,1,0:T(8,128)(2,1)S(1)}, bf16[2,512,640]{2,1,0:T(8,128)(2,1)S(1)}, u32[]{:S(2)}, u32[]{:S(2)}) %collective-permute-start.2) | collective-permute-done | bytes 1310752 | tf_op jit(solution)/shard_map/ppermute | solution.py:138
  174.9 0.1 broadcast_select_fusion.3.refs_6_.refs_7_
  175.1 13.8 %collective-permute-done.21.refs_4_ = bf16[1,512,640]{2,1,0:T(8,128)(2,1)S(1)} collective-permute-done((bf16[1,512,640]{2,1,0:T(8,128)(2,1)S(1)}, bf16[1,512,640]{2,1,0:T(8,128)(2,1)S(1)}, u32[]{:S(2)}, u32[]{:S(2)}) %collective-permute-start.21) | collective-permute-done | bytes 655392 | tf_op jit(solution)/shard_map/ppermute | solution.py:138
  188.9 1.8 collective-permute-start.3
  190.7 12.3 %collective-permute-done.12 = bf16[1,512,640]{2,1,0:T(8,128)(2,1)S(1)} collective-permute-done((bf16[1,512,640]{2,1,0:T(8,128)(2,1)S(1)}, bf16[1,512,640]{2,1,0:T(8,128)(2,1)S(1)}, u32[]{:S(2)}, u32[]{:S(2)}) %collective-permute-start.12) | collective-permute-done | bytes 655392 | tf_op jit(solution)/shard_map/ppermute | solution.py:138
  203.0 9.8 %collective-permute-done.22.refs_5_ = bf16[1,512,640]{2,1,0:T(8,128)(2,1)S(1)} collective-permute-done((bf16[1,512,640]{2,1,0:T(8,128)(2,1)S(1)}, bf16[1,512,640]{2,1,0:T(8,128)(2,1)S(1)}, u32[]{:S(2)}, u32[]{:S(2)}) %collective-permute-start.22) | collective-permute-done | bytes 655392 | tf_op jit(solution)/shard_map/ppermute | solution.py:138
  212.8 18.4 %shard_map.19.refs_7_ = bf16[2,10240,1280]{2,1,0:T(8,128)(2,1)} custom-call(s32[4]{0:T(128)S(1)} %pad_add_fusion.1.owners, bf16[2,512,640]{2,1,0:T(8,128)(2,1)S(1)} %collective-permute-done.19.refs_0_.refs_1_, bf16[2,512,640]{2,1,0:T(8,128)(2,1)S(1)} %collective-permute-done.19.refs_0_.refs_1_, ...), custom_call_target="tpu_custom_call", output_to_operand_aliasing={{}: (10, {})} | custom-call | flops 13421772800 | bytes 23592960 | tf_op jit(solution)/shard_map/pallas_call | solution.py:97
  231.3 1.7 collective-permute-start.4
  233.2 14.4 %shard_map.20.refs_3_ = bf16[2,10240,1280]{2,1,0:T(8,128)(2,1)} custom-call(s32[3]{0:T(128)S(1)} %pad_add_fusion.owners, bf16[1,512,640]{2,1,0:T(8,128)(2,1)S(1)} %broadcast_select_fusion.5.refs_0_, bf16[1,512,640]{2,1,0:T(8,128)(2,1)S(1)} %broadcast_select_fusion.4.refs_1_, ...), custom_call_target="tpu_custom_call", output_to_operand_aliasing={{}: (8, {})} | custom-call | flops 10066329600 | bytes 19005440 | tf_op jit(solution)/shard_map/pallas_call | solution.py:97
  247.5 0.1 collective-permute-done.6.refs_1_
  247.6 5.3 %shard_map.21 = bf16[2,10240,1280]{2,1,0:T(8,128)(2,1)} custom-call(s32[1]{0:T(128)} %bitcast.owners, bf16[1,512,640]{2,1,0:T(8,128)(2,1)S(1)} %collective-permute-done.4.refs_0_, bf16[1,512,640]{2,1,0:T(8,128)(2,1)S(1)} %collective-permute-done.6.refs_1_, ...), custom_call_target="tpu_custom_call", output_to_operand_aliasing={{}: (4, {})} | custom-call | flops 3355443200 | bytes 9830400 | tf_op jit(solution)/shard_map/pallas_call | solution.py:97
  (29 shorter events, 0.6 us)
Async XLA Ops:
  1.5 1.3 copy-start
  3.2 9.8 %collective-permute-start.7 = (bf16[2,512,640]{2,1,0:T(8,128)(2,1)S(1)}, bf16[2,512,640]{2,1,0:T(8,128)(2,1)}, u32[]{:S(2)}, u32[]{:S(2)}) collective-permute-start(bf16[2,512,640]{2,1,0:T(8,128)(2,1)S(1)} %divide_convert_fusion.refs_0_.refs_1_), channel_id=1, source_target_pairs={{0,0},{1,16},{2,1},{3,17},{4,2},{5,18},{6,3},{7,19},{8,4},{9,20},{... | collective-permute-start | bytes 3932168 | tf_op jit(solution)/shard_map/ppermute | solution.py:145
  4.9 61.2 %collective-permute-start.13 = (bf16[2,512,640]{2,1,0:T(8,128)(2,1)S(1)}, bf16[2,512,640]{2,1,0:T(8,128)(2,1)S(1)}, u32[]{:S(2)}, u32[]{:S(2)}) collective-permute-start(bf16[2,512,640]{2,1,0:T(8,128)(2,1)S(1)} %divide_convert_fusion.refs_0_.refs_1_), channel_id=1, source_target_pairs={{0,2},{1,3},{2,0},{3,1},{4,6},{5,7},{6,4},{7,5},{8,10},{9,11},{10,... | collective-permute-start | bytes 3932168 | tf_op jit(solution)/shard_map/ppermute | solution.py:138
  9.6 58.9 %collective-permute-start.9 = (bf16[2,512,640]{2,1,0:T(8,128)(2,1)S(1)}, bf16[2,512,640]{2,1,0:T(8,128)(2,1)}, u32[]{:S(2)}, u32[]{:S(2)}) collective-permute-start(bf16[2,512,640]{2,1,0:T(8,128)(2,1)S(1)} %divide_convert_fusion.refs_0_.refs_1_), channel_id=1, source_target_pairs={{0,1},{1,0},{2,3},{3,2},{4,5},{5,4},{6,7},{7,6},{8,9},{9,8},{10,11... | collective-permute-start | bytes 3932168 | tf_op jit(solution)/shard_map/ppermute | solution.py:138
  9.6 61.4 %collective-permute-start = (bf16[2,512,640]{2,1,0:T(8,128)(2,1)S(1)}, bf16[2,512,640]{2,1,0:T(8,128)(2,1)}, u32[]{:S(2)}, u32[]{:S(2)}) collective-permute-start(bf16[2,512,640]{2,1,0:T(8,128)(2,1)S(1)} %divide_convert_fusion.refs_0_.refs_1_), channel_id=1, source_target_pairs={{0,4},{1,5},{2,6},{3,7},{4,0},{5,1},{6,2},{7,3},{8,12},{9,13},{10,... | collective-permute-start | bytes 3932168 | tf_op jit(solution)/shard_map/ppermute | solution.py:138
  11.2 61.8 %collective-permute-start.17 = (bf16[2,512,640]{2,1,0:T(8,128)(2,1)S(1)}, bf16[2,512,640]{2,1,0:T(8,128)(2,1)}, u32[]{:S(2)}, u32[]{:S(2)}) collective-permute-start(bf16[2,512,640]{2,1,0:T(8,128)(2,1)S(1)} %divide_convert_fusion.refs_0_.refs_1_), channel_id=1, source_target_pairs={{4,8},{5,9},{6,10},{7,11},{8,4},{9,5},{10,6},{11,7},{20,24},{21,25... | collective-permute-start | bytes 3932168 | tf_op jit(solution)/shard_map/ppermute | solution.py:138
  13.0 73.1 %collective-permute-start.8 = (bf16[2,512,640]{2,1,0:T(8,128)(2,1)}, bf16[2,512,640]{2,1,0:T(8,128)(2,1)}, u32[]{:S(2)}, u32[]{:S(2)}) collective-permute-start(bf16[2,512,640]{2,1,0:T(8,128)(2,1)} %collective-permute-done.7), channel_id=1, source_target_pairs={{0,16},{16,0},{1,17},{17,1},{2,18},{18,2},{3,19},{19,3},{4,20},{20... | collective-permute-start | bytes 3932168 | tf_op jit(solution)/shard_map/ppermute | solution.py:146
  67.0 17.8 %collective-permute-start.14 = (bf16[1,512,640]{2,1,0:T(8,128)(2,1)}, bf16[1,512,640]{2,1,0:T(8,128)(2,1)S(1)}, u32[]{:S(2)}, u32[]{:S(2)}) collective-permute-start(bf16[1,512,640]{2,1,0:T(8,128)(2,1)} %slice.43), channel_id=1, source_target_pairs={{0,1},{1,0},{2,3},{3,2},{4,5},{5,4},{6,7},{7,6},{8,9},{9,8},{10,11... | collective-permute-start | bytes 1966088 | tf_op jit(solution)/shard_map/ppermute | solution.py:138
  69.6 20.6 %collective-permute-start.10 = (bf16[1,512,640]{2,1,0:T(8,128)(2,1)S(1)}, bf16[1,512,640]{2,1,0:T(8,128)(2,1)S(1)}, u32[]{:S(2)}, u32[]{:S(2)}) collective-permute-start(bf16[1,512,640]{2,1,0:T(8,128)(2,1)S(1)} %slice.42), channel_id=1, source_target_pairs={{0,2},{1,3},{2,0},{3,1},{4,6},{5,7},{6,4},{7,5},{8,10},{9,11},{10,... | collective-permute-start | bytes 1966088 | tf_op jit(solution)/shard_map/ppermute | solution.py:138
  71.0 68.6 %collective-permute-start.23 = (bf16[2,512,640]{2,1,0:T(8,128)(2,1)}, bf16[2,512,640]{2,1,0:T(8,128)(2,1)S(1)}, u32[]{:S(2)}, u32[]{:S(2)}) collective-permute-start(bf16[2,512,640]{2,1,0:T(8,128)(2,1)} %collective-permute-done.refs_0_.refs_1_), channel_id=1, source_target_pairs={{0,1},{1,0},{2,3},{3,2},{4,5},{5,4},{6,7},{7,6},{8,9},{9,8},{10,11... | collective-permute-start | bytes 3932168 | tf_op jit(solution)/shard_map/ppermute | solution.py:138
  73.0 65.1 %collective-permute-start.1 = (bf16[2,512,640]{2,1,0:T(8,128)(2,1)}, bf16[2,512,640]{2,1,0:T(8,128)(2,1)S(1)}, u32[]{:S(2)}, u32[]{:S(2)}) collective-permute-start(bf16[2,512,640]{2,1,0:T(8,128)(2,1)} %collective-permute-done.refs_0_.refs_1_), channel_id=1, source_target_pairs={{4,8},{5,9},{6,10},{7,11},{8,4},{9,5},{10,6},{11,7},{20,24},{21,25... | collective-permute-start | bytes 3932168 | tf_op jit(solution)/shard_map/ppermute | solution.py:138
  84.7 31.7 %collective-permute-start.18 = (bf16[2,512,640]{2,1,0:T(8,128)(2,1)}, bf16[2,512,640]{2,1,0:T(8,128)(2,1)S(1)}, u32[]{:S(2)}, u32[]{:S(2)}) collective-permute-start(bf16[2,512,640]{2,1,0:T(8,128)(2,1)} %collective-permute-done.17), channel_id=1, source_target_pairs={{4,0},{5,1},{6,2},{7,3},{8,12},{9,13},{10,14},{11,15},{20,16},{21,... | collective-permute-start | bytes 3932168 | tf_op jit(solution)/shard_map/ppermute | solution.py:138
  86.0 31.1 %collective-permute-start.15 = (bf16[1,512,640]{2,1,0:T(8,128)(2,1)S(1)}, bf16[1,512,640]{2,1,0:T(8,128)(2,1)S(1)}, u32[]{:S(2)}, u32[]{:S(2)}) collective-permute-start(bf16[1,512,640]{2,1,0:T(8,128)(2,1)S(1)} %collective-permute-done.14.refs_7_), channel_id=1, source_target_pairs={{4,8},{5,9},{6,10},{7,11},{8,4},{9,5},{10,6},{11,7},{20,24},{21,25... | collective-permute-start | bytes 1966088 | tf_op jit(solution)/shard_map/ppermute | solution.py:138
  90.2 56.6 %collective-permute-start.24 = (bf16[2,512,640]{2,1,0:T(8,128)(2,1)}, bf16[2,512,640]{2,1,0:T(8,128)(2,1)S(1)}, u32[]{:S(2)}, u32[]{:S(2)}) collective-permute-start(bf16[2,512,640]{2,1,0:T(8,128)(2,1)} %collective-permute-done.refs_0_.refs_1_), channel_id=1, source_target_pairs={{0,2},{1,3},{2,0},{3,1},{4,6},{5,7},{6,4},{7,5},{8,10},{9,11},{10,... | collective-permute-start | bytes 3932168 | tf_op jit(solution)/shard_map/ppermute | solution.py:138
  116.4 32.2 %collective-permute-start.11 = (bf16[1,512,640]{2,1,0:T(8,128)(2,1)S(1)}, bf16[1,512,640]{2,1,0:T(8,128)(2,1)S(1)}, u32[]{:S(2)}, u32[]{:S(2)}) collective-permute-start(bf16[1,512,640]{2,1,0:T(8,128)(2,1)S(1)} %collective-permute-done.10.refs_6_), channel_id=1, source_target_pairs={{4,8},{5,9},{6,10},{7,11},{8,4},{9,5},{10,6},{11,7},{20,24},{21,25... | collective-permute-start | bytes 1966088 | tf_op jit(solution)/shard_map/ppermute | solution.py:138
  117.1 31.5 %collective-permute-start.16 = (bf16[1,512,640]{2,1,0:T(8,128)(2,1)S(1)}, bf16[1,512,640]{2,1,0:T(8,128)(2,1)S(1)}, u32[]{:S(2)}, u32[]{:S(2)}) collective-permute-start(bf16[1,512,640]{2,1,0:T(8,128)(2,1)S(1)} %collective-permute-done.15), channel_id=1, source_target_pairs={{4,0},{5,1},{6,2},{7,3},{8,12},{9,13},{10,14},{11,15},{20,16},{21,... | collective-permute-start | bytes 1966088 | tf_op jit(solution)/shard_map/ppermute | solution.py:138
  138.1 36.7 %collective-permute-start.2 = (bf16[2,512,640]{2,1,0:T(8,128)(2,1)S(1)}, bf16[2,512,640]{2,1,0:T(8,128)(2,1)S(1)}, u32[]{:S(2)}, u32[]{:S(2)}) collective-permute-start(bf16[2,512,640]{2,1,0:T(8,128)(2,1)S(1)} %collective-permute-done.1), channel_id=1, source_target_pairs={{4,0},{5,1},{6,2},{7,3},{8,12},{9,13},{10,14},{11,15},{20,16},{21,... | collective-permute-start | bytes 3932168 | tf_op jit(solution)/shard_map/ppermute | solution.py:138
  139.6 49.3 %collective-permute-start.21 = (bf16[1,512,640]{2,1,0:T(8,128)(2,1)S(1)}, bf16[1,512,640]{2,1,0:T(8,128)(2,1)S(1)}, u32[]{:S(2)}, u32[]{:S(2)}) collective-permute-start(bf16[1,512,640]{2,1,0:T(8,128)(2,1)S(1)} %collective-permute-done.10.refs_6_), channel_id=1, source_target_pairs={{0,4},{1,5},{2,6},{3,7},{4,0},{5,1},{6,2},{7,3},{8,12},{9,13},{10,... | collective-permute-start | bytes 1966088 | tf_op jit(solution)/shard_map/ppermute | solution.py:138
  146.8 66.0 %collective-permute-start.19 = (bf16[2,512,640]{2,1,0:T(8,128)(2,1)S(1)}, bf16[2,512,640]{2,1,0:T(8,128)(2,1)S(1)}, u32[]{:S(2)}, u32[]{:S(2)}) collective-permute-start(bf16[2,512,640]{2,1,0:T(8,128)(2,1)S(1)} %broadcast_select_fusion.2.refs_6_.refs_7_), channel_id=1, source_target_pairs={{0,1},{1,0},{2,3},{3,2},{4,5},{5,4},{6,7},{7,6},{8,9},{9,8},{10,11... | collective-permute-start | bytes 3932168 | tf_op jit(solution)/shard_map/ppermute | solution.py:138
  148.6 64.3 %collective-permute-start.20 = (bf16[2,512,640]{2,1,0:T(8,128)(2,1)S(1)}, bf16[2,512,640]{2,1,0:T(8,128)(2,1)S(1)}, u32[]{:S(2)}, u32[]{:S(2)}) collective-permute-start(bf16[2,512,640]{2,1,0:T(8,128)(2,1)S(1)} %broadcast_select_fusion.2.refs_6_.refs_7_), channel_id=1, source_target_pairs={{0,2},{1,3},{2,0},{3,1},{4,6},{5,7},{6,4},{7,5},{8,10},{9,11},{10,... | collective-permute-start | bytes 3932168 | tf_op jit(solution)/shard_map/ppermute | solution.py:138
  148.6 54.4 %collective-permute-start.12 = (bf16[1,512,640]{2,1,0:T(8,128)(2,1)S(1)}, bf16[1,512,640]{2,1,0:T(8,128)(2,1)S(1)}, u32[]{:S(2)}, u32[]{:S(2)}) collective-permute-start(bf16[1,512,640]{2,1,0:T(8,128)(2,1)S(1)} %collective-permute-done.11), channel_id=1, source_target_pairs={{4,0},{5,1},{6,2},{7,3},{8,12},{9,13},{10,14},{11,15},{20,16},{21,... | collective-permute-start | bytes 1966088 | tf_op jit(solution)/shard_map/ppermute | solution.py:138
  174.8 38.0 %collective-permute-start.22 = (bf16[1,512,640]{2,1,0:T(8,128)(2,1)S(1)}, bf16[1,512,640]{2,1,0:T(8,128)(2,1)S(1)}, u32[]{:S(2)}, u32[]{:S(2)}) collective-permute-start(bf16[1,512,640]{2,1,0:T(8,128)(2,1)S(1)} %collective-permute-done.14.refs_7_), channel_id=1, source_target_pairs={{0,4},{1,5},{2,6},{3,7},{4,0},{5,1},{6,2},{7,3},{8,12},{9,13},{10,... | collective-permute-start | bytes 1966088 | tf_op jit(solution)/shard_map/ppermute | solution.py:138
  188.9 42.3 %collective-permute-start.3 = (bf16[2,512,640]{2,1,0:T(8,128)(2,1)S(1)}, bf16[2,512,640]{2,1,0:T(8,128)(2,1)S(1)}, u32[]{:S(2)}, u32[]{:S(2)}) collective-permute-start(bf16[2,512,640]{2,1,0:T(8,128)(2,1)S(1)} %broadcast_select_fusion.3.refs_6_.refs_7_), channel_id=1, source_target_pairs={{0,1},{1,0},{2,3},{3,2},{4,5},{5,4},{6,7},{7,6},{8,9},{9,8},{10,11... | collective-permute-start | bytes 3932168 | tf_op jit(solution)/shard_map/ppermute | solution.py:138
  202.9 30.1 %collective-permute-start.5 = (bf16[2,512,640]{2,1,0:T(8,128)(2,1)S(1)}, bf16[2,512,640]{2,1,0:T(8,128)(2,1)S(1)}, u32[]{:S(2)}, u32[]{:S(2)}) collective-permute-start(bf16[2,512,640]{2,1,0:T(8,128)(2,1)S(1)} %broadcast_select_fusion.3.refs_6_.refs_7_), channel_id=1, source_target_pairs={{0,2},{1,3},{2,0},{3,1},{4,6},{5,7},{6,4},{7,5},{8,10},{9,11},{10,... | collective-permute-start | bytes 3932168 | tf_op jit(solution)/shard_map/ppermute | solution.py:138
  231.3 16.2 %collective-permute-start.4 = (bf16[1,512,640]{2,1,0:T(8,128)(2,1)S(1)}, bf16[1,512,640]{2,1,0:T(8,128)(2,1)S(1)}, u32[]{:S(2)}, u32[]{:S(2)}) collective-permute-start(bf16[1,512,640]{2,1,0:T(8,128)(2,1)S(1)} %slice.38), channel_id=1, source_target_pairs={{0,2},{1,3},{2,0},{3,1},{4,6},{5,7},{6,4},{7,5},{8,10},{9,11},{10,... | collective-permute-start | bytes 1966088 | tf_op jit(solution)/shard_map/ppermute | solution.py:138
  233.1 14.5 %collective-permute-start.6 = (bf16[1,512,640]{2,1,0:T(8,128)(2,1)S(1)}, bf16[1,512,640]{2,1,0:T(8,128)(2,1)S(1)}, u32[]{:S(2)}, u32[]{:S(2)}) collective-permute-start(bf16[1,512,640]{2,1,0:T(8,128)(2,1)S(1)} %slice.39), channel_id=1, source_target_pairs={{0,1},{1,0},{2,3},{3,2},{4,5},{5,4},{6,7},{7,6},{8,9},{9,8},{10,11... | collective-permute-start | bytes 1966088 | tf_op jit(solution)/shard_map/ppermute | solution.py:138
